TPU v7x, 32 devices: a whole 2x2x4 slice. The times are simulated.
32 devices in a mesh: dp: 16 (over z, x, core), tensor: 2 (over y).
Axes of the slice: x: 2, y: 2, z: 4, core: 2. Of those that a mesh axis runs over, the one named last changes fastest.
Arguments:
- tokens: bfloat16 [16384, 1024], P(('dp', 'tensor')), may hold values from -6 to 6
- gains: float32 [2, 1024], replicated, may hold values from 0.5 to 1.5
- shifts: float32 [4, 1024], replicated, may hold values from -1.8 to 1.8
- w_qkv: bfloat16 [1024, 3, 1024], P('dp', None, 'tensor'), may hold values from -0.1875 to 0.1875
- bias_qv: float32 [2, 1024], P(None, 'tensor'), may hold values from -1.8 to 1.8
- w_out: bfloat16 [1024, 1024], P('tensor', 'dp'), may hold values from -1 to 1
- w_in: bfloat16 [1024, 4096], P('dp', 'tensor'), may hold values from -0.1875 to 0.1875
- bias_in: float32 [4096], P('tensor'), may hold values from -1.8 to 1.8
- w_down: bfloat16 [4096, 1024], P('tensor', 'dp'), may hold values from -0.09375 to 0.09375
- segments: int32 [16, 1024], P('dp'), may hold values from 0 to 2, never falling along the last dimension, each value on 1 to 512 neighbouring positions
- grad_output: bfloat16 [16384, 1024], P(('dp', 'tensor')), may hold values from -6 to 6
Outputs:
- output: bfloat16 [16384, 1024], P(('dp', 'tensor'))
- input_grad: bfloat16 [16384, 1024], P(('dp', 'tensor'))
- gains_grad: float32 [2, 1024], P(None, ('dp', 'tensor'))
- shifts_grad: float32 [4, 1024], P(None, ('dp', 'tensor'))
- w_qkv_grad: float32 [1024, 3, 1024], P('dp', None, 'tensor')
- bias_qv_grad: float32 [2, 1024], P(None, ('tensor', 'dp'))
- w_out_grad: float32 [1024, 1024], P('tensor', 'dp')
- w_in_grad: float32 [1024, 4096], P('dp', 'tensor')
- bias_in_grad: float32 [4096], P(('tensor', 'dp'))
- w_down_grad: float32 [4096, 1024], P('tensor', 'dp')
Inputs may be any that keep to these rules, and one draw needn't show every extreme that they name: `segments`: along each sequence the numbers never fall; each document spans 1 to 512 tokens.
All inputs are finite; a program needn't handle non-finite values.
Results may differ from a plain program's by a relative error of at most 0.02.
Values may be sent and summed in bfloat16 or wider, within the bound.
A program may use at most 192 MiB of HBM per device.

v0:
```python
import math
import jax
import jax.numpy as jnp
from jax import lax
from jax.sharding import PartitionSpec as P

HEAD_DIM = 64
EPS = 1e-05
MASKED = -1000000000.0
GELU_C = 0.7978845608028654


def layer_norm(value, gain, shift):
    centre = value - jnp.mean(value, axis=-1, keepdims=True)
    spread = jnp.mean(centre * centre, axis=-1, keepdims=True)
    return centre * lax.rsqrt(spread + EPS) * gain + shift


def gelu_tanh(value):
    return 0.5 * value * (1.0 + jnp.tanh(GELU_C * (value + 0.044715 * value * value * value)))


def xor_send(value, axis, distance):
    size = lax.axis_size(axis)
    return lax.ppermute(value, axis, [(i, i ^ distance) for i in range(size)])


def join_shards(*shards):
    widths = [shard.shape[1] for shard in shards]
    full = lax.all_gather(jnp.concatenate(shards, axis=1), "dp", axis=0, tiled=True)
    parts = []
    start = 0
    for width in widths:
        parts.append(full[:, start : start + width])
        start += width
    return parts


def spread_rows(rows):
    blocks = [rows] + [xor_send(rows, "tensor", d) for d in range(1, lax.axis_size("tensor"))]
    return jnp.concatenate(blocks, axis=0)


def to_natural(values):
    ranks = lax.axis_size("tensor")
    me = lax.axis_index("tensor")
    rows = values.shape[0] // ranks
    if ranks == 2:
        own, other = (values[:rows], values[rows:])
        return jnp.concatenate(
            [jnp.where(me == 0, own, other), jnp.where(me == 0, other, own)], axis=0
        )
    blocks = values.reshape(ranks, rows, *values.shape[1:])
    picked = [
        lax.dynamic_index_in_dim(blocks, jnp.bitwise_xor(me, j), 0, keepdims=False)
        for j in range(ranks)
    ]
    return jnp.concatenate(picked, axis=0)


def sum_to_owner(product, values):
    ranks = lax.axis_size("tensor")
    rows = values.shape[0] // ranks
    arrived = []
    for distance in range(1, ranks):
        part = product(values[distance * rows : (distance + 1) * rows]).astype(jnp.bfloat16)
        arrived.append(xor_send(part, "tensor", distance))
    total = product(values[:rows])
    for part in arrived:
        total = total + part.astype(jnp.float32)
    return total


def times(weight):
    return lambda rows: jnp.dot(rows, weight, preferred_element_type=jnp.float32)


def times_transposed(weight):
    return lambda rows: lax.dot_general(
        rows, weight, (((1,), (1,)), ((), ())), preferred_element_type=jnp.float32
    )


def halving_sum(value, axis, order, keep_dtype):
    size = lax.axis_size(axis)
    me = lax.axis_index(axis)
    left = [bit for bit in reversed(range(len(order)))]
    tail = (value.shape[0] // size,) + value.shape[1:]
    value = value.reshape((2,) * len(order) + tail)
    for step, bit in enumerate(order):
        place = left.index(bit)
        left.remove(bit)
        mine = lax.rem(me // (1 << bit), 2)
        send = lax.dynamic_index_in_dim(value, 1 - mine, place, keepdims=False)
        keep = lax.dynamic_index_in_dim(value, mine, place, keepdims=False)
        got = xor_send(send, axis, 1 << bit)
        value = keep.astype(jnp.float32) + got.astype(jnp.float32)
        if step < len(order) - 1:
            value = value.astype(keep_dtype)
    return value


def dp_orders():
    bits = lax.axis_size("dp").bit_length() - 1
    ahead = list(range(bits))
    return (ahead, [0] + ahead[2:] + ahead[1:2])


def dp_sum(value, order):
    return halving_sum(value.astype(jnp.bfloat16), "dp", order, jnp.bfloat16)


def masks_for(seg, start, end):
    positions = jnp.arange(end, dtype=jnp.int32)
    same = seg[start:end, None] == seg[None, :end]
    causal = positions[start:end, None] >= positions[None, :end]
    return same & causal


def attention_forward(query, key, value, segments, scale):
    length = query.shape[1]
    block = min(512, length)
    blocks = length // block

    def one_seq(items):
        q_seq, k_seq, v_seq, seg = items
        outs = []
        sums = []
        for index in range(blocks):
            start = index * block
            end = start + block
            allowed = masks_for(seg, start, end)
            scores = (
                jnp.einsum(
                    "qhd,khd->hqk",
                    q_seq[start:end],
                    k_seq[:end],
                    preferred_element_type=jnp.float32,
                )
                * scale
            )
            scores = jnp.where(allowed[None], scores, MASKED)
            top = jnp.max(scores, axis=-1, keepdims=True)
            expo = jnp.exp(scores - top)
            total = jnp.sum(expo, axis=-1, keepdims=True)
            probs = (expo / total).astype(jnp.bfloat16)
            outs.append(
                jnp.einsum("hqk,khd->qhd", probs, v_seq[:end], preferred_element_type=jnp.float32)
            )
            sums.append((top + jnp.log(total))[..., 0])
        return (jnp.concatenate(outs, 0), jnp.concatenate(sums, 1))

    return lax.map(one_seq, (query, key, value, segments))


def attention_backward(query, key, value, segments, logsum, grad_att, scale):
    length = query.shape[1]
    block = min(512, length)
    blocks = length // block

    def one_seq(items):
        q_seq, k_seq, v_seq, seg, lse, do_seq = items
        dq_parts = []
        key_grad = jnp.zeros(k_seq.shape, jnp.float32)
        value_grad = jnp.zeros(v_seq.shape, jnp.float32)
        for index in range(blocks):
            start = index * block
            end = start + block
            allowed = masks_for(seg, start, end)
            q_rows = q_seq[start:end]
            do_rows = do_seq[start:end]
            scores = (
                jnp.einsum("qhd,khd->hqk", q_rows, k_seq[:end], preferred_element_type=jnp.float32)
                * scale
            )
            scores = jnp.where(allowed[None], scores, MASKED)
            probs = jnp.exp(scores - lse[:, start:end, None])
            probs_low = probs.astype(jnp.bfloat16)
            dprobs = jnp.einsum(
                "qhd,khd->hqk", do_rows, v_seq[:end], preferred_element_type=jnp.float32
            )
            inner = jnp.sum(dprobs * probs, axis=-1, keepdims=True)
            dscores = (probs * (dprobs - inner)).astype(jnp.bfloat16)
            dq_parts.append(
                jnp.einsum("hqk,khd->qhd", dscores, k_seq[:end], preferred_element_type=jnp.float32)
                * scale
            )
            key_grad = key_grad.at[:end].add(
                jnp.einsum("hqk,qhd->khd", dscores, q_rows, preferred_element_type=jnp.float32)
                * scale
            )
            value_grad = value_grad.at[:end].add(
                jnp.einsum("hqk,qhd->khd", probs_low, do_rows, preferred_element_type=jnp.float32)
            )
        return (jnp.concatenate(dq_parts, 0), key_grad, value_grad)

    return lax.map(one_seq, (query, key, value, segments, logsum, grad_att))


def per_device(
    tokens, gains, shifts, w_qkv, bias_qv, w_out, w_in, bias_in, w_down, segments, grad_output
):
    seqs, length = segments.shape
    scale = 1.0 / math.sqrt(HEAD_DIM)
    order_a, order_b = dp_orders()
    shard = w_qkv.shape[0]
    local_width = w_qkv.shape[2]
    ranks = lax.axis_size("tensor")
    my_rank = lax.axis_index("tensor")
    rows_local = tokens.shape[0]
    qkv_flat, out_turned = join_shards(w_qkv.reshape(shard, 3 * local_width), w_out.T)
    in_full, down_turned = join_shards(w_in, w_down.T)
    heads = local_width // HEAD_DIM
    rows_in = tokens.astype(jnp.float32)
    normed_one = layer_norm(rows_in, gains[0], shifts[0])
    full_a = spread_rows(normed_one.astype(jnp.bfloat16))
    full_dy = spread_rows(grad_output)
    total = full_a.shape[0]
    bias_all = jnp.concatenate([bias_qv[0], jnp.zeros_like(bias_qv[0]), bias_qv[1]])
    mixed = jnp.dot(full_a, qkv_flat, preferred_element_type=jnp.float32) + bias_all
    shaped = to_natural(mixed.astype(jnp.bfloat16)).reshape(seqs, length, 3, heads, HEAD_DIM)
    query = shaped[:, :, 0]
    key = shaped[:, :, 1]
    value = shaped[:, :, 2]
    attended, logsum = attention_forward(query, key, value, segments, scale)
    attended_low = to_natural(attended.reshape(total, local_width).astype(jnp.bfloat16))
    middle = rows_in + sum_to_owner(times_transposed(out_turned), attended_low) + shifts[1]
    normed_two = layer_norm(middle, gains[1], shifts[2])
    full_m = spread_rows(normed_two.astype(jnp.bfloat16))
    hidden_grad = jnp.dot(full_dy, down_turned, preferred_element_type=jnp.float32)
    hidden_pre = jnp.dot(full_m, in_full, preferred_element_type=jnp.float32) + bias_in
    hidden_low = gelu_tanh(hidden_pre).astype(jnp.bfloat16)
    gelu_out, gelu_back = jax.vjp(gelu_tanh, hidden_pre)
    pre_grad = gelu_back(hidden_grad)[0].astype(jnp.bfloat16)
    normed_two_grad = sum_to_owner(times_transposed(in_full), pre_grad)
    result = middle + sum_to_owner(times_transposed(down_turned), hidden_low) + shifts[3]
    output = result.astype(jnp.bfloat16)
    grad_rows = grad_output.astype(jnp.float32)
    bias_in_part = jnp.sum(pre_grad, axis=0, dtype=jnp.float32)
    down_grad = lax.dot_general(
        full_dy, hidden_low, (((0,), (0,)), ((), ())), preferred_element_type=jnp.float32
    )
    in_grad = lax.dot_general(
        full_m, pre_grad, (((0,), (0,)), ((), ())), preferred_element_type=jnp.float32
    )
    ff_in = dp_sum(in_grad, order_a)
    ff_down = dp_sum(down_grad, order_b).T
    norm_two_out, norm_two_back = jax.vjp(layer_norm, middle, gains[1], shifts[2])
    middle_part, gain_two_grad, shift_two_grad = norm_two_back(normed_two_grad)
    middle_grad = grad_rows + middle_part
    branch_low = middle_grad.astype(jnp.bfloat16)
    full_branch = spread_rows(branch_low)
    attended_grad = jnp.dot(full_branch, out_turned, preferred_element_type=jnp.float32)
    attended_grad_low = to_natural(attended_grad.astype(jnp.bfloat16))
    out_grad = lax.dot_general(
        full_branch, attended_low, (((0,), (0,)), ((), ())), preferred_element_type=jnp.float32
    )
    att_out = dp_sum(out_grad, order_b).T
    query_grad, key_grad, value_grad = attention_backward(
        query,
        key,
        value,
        segments,
        logsum,
        attended_grad_low.reshape(seqs, length, heads, HEAD_DIM),
        scale,
    )
    mixed_grad = jnp.concatenate(
        [
            part.astype(jnp.bfloat16).reshape(total, local_width)
            for part in (query_grad, key_grad, value_grad)
        ],
        axis=1,
    )
    mixed_flat = to_natural(mixed_grad)
    normed_one_grad = sum_to_owner(times_transposed(qkv_flat), mixed_flat)
    qkv_grad = lax.dot_general(
        full_a, mixed_flat, (((0,), (0,)), ((), ())), preferred_element_type=jnp.float32
    )
    half = 3 * local_width // 2
    att_qkv = jnp.concatenate(
        [dp_sum(qkv_grad[:, :half], order_a), dp_sum(qkv_grad[:, half:], order_b)], axis=1
    ).reshape(shard, 3, local_width)
    mixed_bias = jnp.sum(mixed_flat, axis=0, dtype=jnp.float32)
    bias_qv_part = jnp.stack([mixed_bias[:local_width], mixed_bias[2 * local_width :]])
    norm_one_out, norm_one_back = jax.vjp(layer_norm, rows_in, gains[0], shifts[0])
    input_part, gain_one_grad, shift_one_grad = norm_one_back(normed_one_grad)
    input_grad = (middle_grad + input_part).astype(jnp.bfloat16)
    norm_parts = jnp.stack(
        [
            gain_one_grad,
            gain_two_grad,
            shift_one_grad,
            jnp.sum(branch_low, axis=0, dtype=jnp.float32),
            shift_two_grad,
            jnp.sum(grad_rows, axis=0),
        ]
    )
    groups = lax.axis_size("dp")
    width = norm_parts.shape[1] // (groups * ranks)
    norm_packed = norm_parts.reshape(6, groups, ranks, width).transpose(1, 2, 0, 3)
    norm_packed = norm_packed.reshape(groups, ranks, 6 * width)
    bias_packed = jnp.concatenate(
        [
            bias_qv_part.reshape(2, groups, -1).transpose(1, 0, 2).reshape(groups, -1),
            bias_in_part.reshape(groups, -1),
        ],
        axis=1,
    )
    mine = jnp.arange(ranks, dtype=jnp.int32)[None, :, None] == my_rank
    bias_spread = jnp.where(mine, bias_packed[:, None, :], 0.0)
    packed = jnp.concatenate([norm_packed, bias_spread], axis=2)
    packed = packed.transpose(1, 0, 2)
    rank_bits = list(range(ranks.bit_length() - 1))
    summed = halving_sum(packed, "tensor", rank_bits, jnp.float32)[0]
    summed = halving_sum(summed, "dp", order_a, jnp.float32)[0]
    norm_sums = summed[: 6 * width].reshape(6, width)
    gains_grad, shifts_grad = (norm_sums[:2], norm_sums[2:])
    qv_width = bias_qv_part.shape[1] // groups
    att_bias = summed[6 * width : 6 * width + 2 * qv_width].reshape(2, qv_width)
    ff_bias = summed[6 * width + 2 * qv_width :]
    return (
        output,
        input_grad,
        gains_grad,
        shifts_grad,
        att_qkv,
        att_bias,
        att_out,
        ff_in,
        ff_bias,
        ff_down,
    )


def solution(mesh):
    placed = (
        P(("dp", "tensor"), None),
        P(),
        P(),
        P("dp", None, "tensor"),
        P(None, "tensor"),
        P("tensor", "dp"),
        P("dp", "tensor"),
        P("tensor"),
        P("tensor", "dp"),
        P("dp", None),
        P(("dp", "tensor"), None),
    )
    return jax.shard_map(
        per_device,
        mesh=mesh,
        in_specs=placed,
        out_specs=(
            P(("dp", "tensor"), None),
            P(("dp", "tensor"), None),
            P(None, ("dp", "tensor")),
            P(None, ("dp", "tensor")),
            P("dp", None, "tensor"),
            P(None, ("tensor", "dp")),
            P("tensor", "dp"),
            P("dp", "tensor"),
            P(("tensor", "dp")),
            P("tensor", "dp"),
        ),
        check_vma=False,
    )
```

profile of v0, /device:TPU:0, one launch (start us, length us, event | category | flops | bytes accessed | tf_op | source)
XLA Modules:
  0.0 490.9 jit_solution(2536031003911943238)
XLA Ops:
  18.3 21.5 %collective-permute-done = bf16[512,1024]{1,0:T(8,128)(2,1)S(1)} collective-permute-done((bf16[512,1024]{1,0:T(8,128)(2,1)S(1)}, bf16[512,1024]{1,0:T(8,128)(2,1)S(1)}, u32[]{:S(2)}, u32[]{:S(2)}) %collective-permute-start) | collective-permute-done | bytes 1048608 | tf_op jit(solution)/shard_map/ppermute | solution.py:25
  39.8 24.3 %all-gather.3.cloned.1.call-done = bf16[1024,2048]{1,0:T(8,128)(2,1)} async-done(((bf16[64,2048]{1,0:T(8,128)(2,1)}), bf16[1024,2048]{1,0:T(8,128)(2,1)}) %all-gather.3.cloned.1.call-update) | async-done | bytes 4194320 | tf_op jit(solution)/shard_map/all_gather | solution.py:30
  64.1 6.8 %add_convert_fusion = bf16[1024,1536]{1,0:T(8,128)(2,1)S(1)} fusion(f32[1536]{0:T(1024)S(1)} %pad_maximum_fusion.17, bf16[1024,2048]{1,0:T(8,128)(2,1)} %all-gather.3.cloned.1.call-done, bf16[512,1024]{1,0:T(8,128)(2,1)S(1)} %collective-permute-done, bf16[512,1024]{1,0:T(8,128)(2,1)S(1)} %fusion.46), kind=kOutput, calls=%fused_computation.32 | convolution fusion | flops 3228565504 | bytes 8394752 | tf_op jit(solution)/shard_map/dot_general | solution.py:220
  86.1 3.5 fusion
  92.8 5.3 %fusion.85 = bf16[8,64,512]{2,1,0:T(8,128)(2,1)} fusion(f32[8,512,1024]{2,1,0:T(8,128)S(1)} %get-tuple-element.219, f32[8,512]{1,0:T(8,128)S(1)} %fusion, f32[8,512]{1,0:T(8,128)S(1)} %get-tuple-element.218, bf16[1,1024,3,8,64]{1,4,3,2,0:T(8,128)(2,1)} %bitcast.269), kind=kOutput, calls=%fused_computation.135 | convolution fusion | flops 549715968 | bytes 18382848 | tf_op jit(solution)/shard_map/while/body/eval_jaxpr/hqk,khd->qhd/dot_general | solution.py:148
  98.1 3.3 broadcast_select_fusion.5
  104.5 24.0 %collective-permute-done.1 = bf16[512,1024]{1,0:T(8,128)(2,1)S(1)} collective-permute-done((bf16[512,1024]{1,0:T(8,128)(2,1)S(1)}, bf16[512,1024]{1,0:T(8,128)(2,1)S(1)}, u32[]{:S(2)}, u32[]{:S(2)}) %collective-permute-start.1) | collective-permute-done | bytes 1048608 | tf_op jit(solution)/shard_map/ppermute | solution.py:25
  133.4 17.5 %collective-permute-done.4 = bf16[512,1024]{1,0:T(8,128)(2,1)S(1)} collective-permute-done((bf16[512,1024]{1,0:T(8,128)(2,1)S(1)}, bf16[512,1024]{1,0:T(8,128)(2,1)S(1)}, u32[]{:S(2)}, u32[]{:S(2)}) %collective-permute-start.4) | collective-permute-done | bytes 1048608 | tf_op jit(solution)/shard_map/ppermute | solution.py:25
  153.0 19.8 %collective-permute-done.2 = bf16[512,1024]{1,0:T(8,128)(2,1)} collective-permute-done((bf16[512,1024]{1,0:T(8,128)(2,1)S(1)}, bf16[512,1024]{1,0:T(8,128)(2,1)}, u32[]{:S(2)}, u32[]{:S(2)}) %collective-permute-start.2) | collective-permute-done | bytes 1048608 | tf_op jit(solution)/shard_map/ppermute | solution.py:25
  172.8 10.2 %multiply_convert_fusion.2 = (bf16[1024,2048]{1,0:T(8,128)(2,1)S(1)}, f32[1024,2048]{1,0:T(8,128)}) fusion(f32[2048]{0:T(1024)S(1)} %copy-done.69, bf16[1024,4096]{1,0:T(8,128)(2,1)} %all-gather.5.cloned.1.call-done, bf16[512,1024]{1,0:T(8,128)(2,1)} %collective-permute-done.2, bf16[512,1024]{1,0:T(8,128)(2,1)S(1)} %add_convert_fusion.3), kind=kOutput, calls=%fused_computation.24 | convolution fusion | flops 4320133120 | bytes 18882560 | tf_op jit(solution)/shard_map/dot_general | solution.py:231
  183.0 3.4 fusion.72
  188.0 4.9 convolution_convert_fusion.1
  192.8 13.2 %convert_reduce_fusion = (f32[2048]{0:T(1024)S(1)}, bf16[1024,2048]{1,0:T(8,128)(2,1)S(1)}) fusion(bf16[1024,1024]{1,0:T(8,128)(2,1)S(1)} %copy-done.31, bf16[1024,4096]{1,0:T(8,128)(2,1)S(1)} %copy-done.62, f32[1024,2048]{1,0:T(8,128)} %get-tuple-element.224, f32[2048]{0:T(1024)S(1)} %copy-done.69), kind=kOutput, calls=%fused_computation.19 | convolution fusion | flops 4351588352 | bytes 18890752 | tf_op jit(solution)/shard_map/dot_general | solution.py:230
  209.0 6.5 %convolution_convert_fusion.2 = bf16[1024,2048]{1,0:T(8,128)(2,1)S(1)} fusion(bf16[1024,2048]{1,0:T(8,128)(2,1)S(1)} %get-tuple-element.231, bf16[512,1024]{1,0:T(8,128)(2,1)} %collective-permute-done.2, bf16[512,1024]{1,0:T(8,128)(2,1)S(1)} %add_convert_fusion.3), kind=kOutput, calls=%fused_computation.42 | convolution fusion | flops 4301258752 | bytes 10485760 | tf_op jit(solution)/shard_map/dot_general | solution.py:243
  221.5 12.1 %collective-permute-done.5 = bf16[512,1024]{1,0:T(8,128)(2,1)S(1)} collective-permute-done((bf16[512,1024]{1,0:T(8,128)(2,1)S(1)}, bf16[512,1024]{1,0:T(8,128)(2,1)S(1)}, u32[]{:S(2)}, u32[]{:S(2)}) %collective-permute-start.5) | collective-permute-done | bytes 1048608 | tf_op jit(solution)/shard_map/ppermute | solution.py:25
  233.6 6.9 %multiply_reduce_fusion.2 = (f32[1024]{0:T(1024)S(1)}, f32[512]{0:T(512)S(1)}, f32[1024]{0:T(1024)S(1)}, f32[512,1024]{1,0:T(8,128)}) fusion(f32[512,1024]{1,0:T(8,128)S(1)} %copy-done.13, f32[512]{0:T(512)S(1)} %fusion.126, f32[512]{0:T(512)S(1)} %broadcast_multiply_fusion, bf16[512,1024]{1,0:T(8,128)(2,1)S(1)} %collective-permute-done.5, ...), kind=kOutput, calls=%fused_computation.102 | convolution fusion | flops 2152723968 | bytes 11552768 | tf_op jit(solution)/shard_map/dot_general | solution.py:79
  241.9 8.4 %fusion.138 = (f32[512]{0:T(512)S(1)}, f32[512,1024]{1,0:T(8,128)S(1)}, bf16[512,1024]{1,0:T(8,128)(2,1)}) fusion(f32[512]{0:T(512)S(1)} %multiply_multiply_fusion.3, f32[512,1024]{1,0:T(8,128)} %copy-done.12, f32[512]{0:T(512)S(1)} %broadcast_multiply_fusion, f32[512]{0:T(512)S(1)} %fusion.126, f32[1024]{0:T(1024)S(1)} %bitcast.307, ...), kind=kOutput, calls=%fused_computation.284 | convolution fusion | flops 2154823168 | bytes 15745024 | tf_op jit(solution)/shard_map/dot_general | solution.py:79
  264.9 13.1 %collective-permute-done.6 = bf16[512,1024]{1,0:T(8,128)(2,1)S(1)} collective-permute-done((bf16[512,1024]{1,0:T(8,128)(2,1)}, bf16[512,1024]{1,0:T(8,128)(2,1)S(1)}, u32[]{:S(2)}, u32[]{:S(2)}) %collective-permute-start.6) | collective-permute-done | bytes 1048608 | tf_op jit(solution)/shard_map/ppermute | solution.py:25
  293.4 3.6 fusion.80
  300.2 10.1 %multiply_reduce_fusion = (f32[8,512]{1,0:T(8,128)}, f32[8,512,1024]{2,1,0:T(8,128)}) fusion(f32[8,512,1024]{2,1,0:T(8,128)S(1)} %bitcast.265, f32[8,512]{1,0:T(8,128)} %log_add_fusion, bf16[512,8,64]{0,2,1:T(8,128)(2,1)} %bitcast.281, bf16[1,1024,3,8,64]{1,4,3,2,0:T(8,128)(2,1)} %bitcast.274), kind=kOutput, calls=%fused_computation.1 | convolution fusion | flops 549449728 | bytes 35160064 | tf_op jit(solution)/shard_map/while/body/eval_jaxpr/qhd,khd->hqk/dot_general | solution.py:179
  310.3 5.0 %fusion.57 = bf16[1024,8,64]{0,2,1:T(8,128)(2,1)} fusion(f32[512,8,64]{0,2,1:T(8,128)} %fusion.77, bf16[512,8,64]{0,2,1:T(8,128)(2,1)} %bitcast.282, f32[8,512,1024]{2,1,0:T(8,128)S(1)} %bitcast.265, f32[8,512]{1,0:T(8,128)} %log_add_fusion), kind=kOutput, calls=%fused_computation.96 | convolution fusion | flops 546308096 | bytes 19415040 | tf_op jit(solution)/shard_map/while/body/eval_jaxpr/hqk,qhd->khd/dot_general | solution.py:193
  318.8 11.9 %multiply_convert_fusion = bf16[8,512,1024]{2,1,0:T(8,128)(2,1)S(1)} fusion(f32[8,512,1024]{2,1,0:T(8,128)} %get-tuple-element.228, f32[8,512,1024]{2,1,0:T(8,128)} %copy-done, f32[8,512]{1,0:T(8,128)S(1)} %copy-done.41, f32[8,512]{1,0:T(8,128)S(1)} %copy-done.33), kind=kLoop, calls=%fused_computation | loop fusion | flops 16777216 | bytes 41975808 | tf_op jit(solution)/shard_map/while/body/eval_jaxpr/convert_element_type | solution.py:183
  330.8 3.5 fusion.82
  343.6 5.5 %convolution_convert_fusion = bf16[1024,1536]{1,0:T(8,128)(2,1)S(1)} fusion(bf16[512,1536]{1,0:T(8,128)(2,1)} %copy-done.16, bf16[512,1536]{1,0:T(8,128)(2,1)S(1)} %get-tuple-element.186, bf16[512,1024]{1,0:T(8,128)(2,1)} %copy-done.65, bf16[512,1024]{1,0:T(8,128)(2,1)} %copy-done.29), kind=kOutput, calls=%fused_computation.40 | convolution fusion | flops 3233284096 | bytes 8388608 | tf_op jit(solution)/shard_map/dot_general | solution.py:277
  353.0 3.8 fusion.64
  360.5 6.3 %collective-permute-done.22 = bf16[2,2,64,512]{3,2,1,0:T(8,128)(2,1)S(1)} collective-permute-done((bf16[2,2,64,512]{3,2,1,0:T(8,128)(2,1)S(1)}, bf16[2,2,64,512]{3,2,1,0:T(8,128)(2,1)S(1)}, u32[]{:S(2)}, u32[]{:S(2)}) %collective-permute-start.22) | collective-permute-done | bytes 262176 | tf_op jit(solution)/shard_map/ppermute | solution.py:25
  372.5 3.6 collective-permute-done.23
  376.8 14.6 %collective-permute-done.7 = bf16[512,1024]{1,0:T(8,128)(2,1)S(1)} collective-permute-done((bf16[512,1024]{1,0:T(8,128)(2,1)S(1)}, bf16[512,1024]{1,0:T(8,128)(2,1)S(1)}, u32[]{:S(2)}, u32[]{:S(2)}) %collective-permute-start.7) | collective-permute-done | bytes 1048608 | tf_op jit(solution)/shard_map/ppermute | solution.py:25
  414.4 10.2 %collective-permute-done.11 = f32[2,1,384]{2,1,0:T(1,128)S(1)} collective-permute-done((f32[2,1,384]{2,1,0:T(1,128)S(1)}, f32[2,1,384]{2,1,0:T(1,128)S(1)}, u32[]{:S(2)}, u32[]{:S(2)}) %collective-permute-start.11) | collective-permute-done | bytes 3104 | tf_op jit(solution)/shard_map/ppermute | solution.py:25
  436.6 7.8 %collective-permute-done.15 = bf16[2,64,768]{2,1,0:T(8,128)(2,1)S(1)} collective-permute-done((bf16[2,64,768]{2,1,0:T(8,128)(2,1)S(1)}, bf16[2,64,768]{2,1,0:T(8,128)(2,1)S(1)}, u32[]{:S(2)}, u32[]{:S(2)}) %collective-permute-start.15) | collective-permute-done | bytes 196640 | tf_op jit(solution)/shard_map/ppermute | solution.py:25
  447.2 15.0 %collective-permute-done.19 = bf16[2,64,768]{2,1,0:T(8,128)(2,1)S(1)} collective-permute-done((bf16[2,64,768]{2,1,0:T(8,128)(2,1)S(1)}, bf16[2,64,768]{2,1,0:T(8,128)(2,1)S(1)}, u32[]{:S(2)}, u32[]{:S(2)}) %collective-permute-start.19) | collective-permute-done | bytes 196640 | tf_op jit(solution)/shard_map/ppermute | solution.py:25
  469.8 12.4 %collective-permute-done.28 = bf16[64,2048]{1,0:T(8,128)(2,1)S(1)} collective-permute-done((bf16[64,2048]{1,0:T(8,128)(2,1)S(1)}, bf16[64,2048]{1,0:T(8,128)(2,1)S(1)}, u32[]{:S(2)}, u32[]{:S(2)}) %collective-permute-start.28) | collective-permute-done | bytes 262176 | tf_op jit(solution)/shard_map/ppermute | solution.py:25
  (368 shorter events, 157.6 us)
Async XLA Ops:
  7.2 56.9 %all-gather.3.cloned.1.call-start = ((), (), s32[]{:S(2)}) async-start(), calls=%async_computation | async-start | bytes 4456448 | tf_op jit(solution)/shard_map/all_gather | solution.py:30
  9.9 163.0 %all-gather.5.cloned.1.call-start = ((), (), s32[]{:S(2)}) async-start(), calls=%async_computation.1 | async-start | bytes 8912896 | tf_op jit(solution)/shard_map/all_gather | solution.py:30
  13.6 26.2 %collective-permute-start = (bf16[512,1024]{1,0:T(8,128)(2,1)S(1)}, bf16[512,1024]{1,0:T(8,128)(2,1)S(1)}, u32[]{:S(2)}, u32[]{:S(2)}) collective-permute-start(bf16[512,1024]{1,0:T(8,128)(2,1)S(1)} %fusion.46), channel_id=1, source_target_pairs={{0,1},{1,0},{2,3},{3,2},{4,5},{5,4},{6,7},{7,6},{8,9},{9,8},{10,11... | collective-permute-start | bytes 3145736 | tf_op jit(solution)/shard_map/ppermute | solution.py:25
  102.4 26.1 %collective-permute-start.1 = (bf16[512,1024]{1,0:T(8,128)(2,1)S(1)}, bf16[512,1024]{1,0:T(8,128)(2,1)S(1)}, u32[]{:S(2)}, u32[]{:S(2)}) collective-permute-start(bf16[512,1024]{1,0:T(8,128)(2,1)S(1)} %convolution_convert_fusion.5), channel_id=1, source_target_pairs={{0,1},{1,0},{2,3},{3,2},{4,5},{5,4},{6,7},{7,6},{8,9},{9,8},{10,11... | collective-permute-start | bytes 3145736 | tf_op jit(solution)/shard_map/ppermute | solution.py:25
  104.0 46.9 %collective-permute-start.4 = (bf16[512,1024]{1,0:T(8,128)(2,1)S(1)}, bf16[512,1024]{1,0:T(8,128)(2,1)S(1)}, u32[]{:S(2)}, u32[]{:S(2)}) collective-permute-start(bf16[512,1024]{1,0:T(8,128)(2,1)S(1)} %copy-done.8), channel_id=1, source_target_pairs={{0,1},{1,0},{2,3},{3,2},{4,5},{5,4},{6,7},{7,6},{8,9},{9,8},{10,11... | collective-permute-start | bytes 3145736 | tf_op jit(solution)/shard_map/ppermute | solution.py:25
  131.2 41.6 %collective-permute-start.2 = (bf16[512,1024]{1,0:T(8,128)(2,1)S(1)}, bf16[512,1024]{1,0:T(8,128)(2,1)}, u32[]{:S(2)}, u32[]{:S(2)}) collective-permute-start(bf16[512,1024]{1,0:T(8,128)(2,1)S(1)} %add_convert_fusion.3), channel_id=1, source_target_pairs={{0,1},{1,0},{2,3},{3,2},{4,5},{5,4},{6,7},{7,6},{8,9},{9,8},{10,11... | collective-permute-start | bytes 3145736 | tf_op jit(solution)/shard_map/ppermute | solution.py:25
  186.4 55.4 %collective-permute-start.3 = (bf16[512,1024]{1,0:T(8,128)(2,1)}, bf16[512,1024]{1,0:T(8,128)(2,1)}, u32[]{:S(2)}, u32[]{:S(2)}) collective-permute-start(bf16[512,1024]{1,0:T(8,128)(2,1)} %fusion.72), channel_id=1, source_target_pairs={{0,1},{1,0},{2,3},{3,2},{4,5},{5,4},{6,7},{7,6},{8,9},{9,8},{10,11... | collective-permute-start | bytes 3145736 | tf_op jit(solution)/shard_map/ppermute | solution.py:25
  208.4 25.2 %collective-permute-start.5 = (bf16[512,1024]{1,0:T(8,128)(2,1)S(1)}, bf16[512,1024]{1,0:T(8,128)(2,1)S(1)}, u32[]{:S(2)}, u32[]{:S(2)}) collective-permute-start(bf16[512,1024]{1,0:T(8,128)(2,1)S(1)} %fusion.67), channel_id=1, source_target_pairs={{0,1},{1,0},{2,3},{3,2},{4,5},{5,4},{6,7},{7,6},{8,9},{9,8},{10,11... | collective-permute-start | bytes 3145736 | tf_op jit(solution)/shard_map/ppermute | solution.py:25
  221.0 34.1 %collective-permute-start.25 = (bf16[2,2,2,64,2048]{4,3,0,1,2:T(8,128)(2,1)}, bf16[2,2,2,64,2048]{4,3,0,1,2:T(8,128)(2,1)}, u32[]{:S(2)}, u32[]{:S(2)}) collective-permute-start(bf16[2,2,2,64,2048]{4,3,0,1,2:T(8,128)(2,1)} %bitcast.259), channel_id=1, source_target_pairs={{0,2},{2,0},{4,6},{6,4},{8,10},{10,8},{12,14},{14,12},{16,18},{18,... | collective-permute-start | bytes 6291464 | tf_op jit(solution)/shard_map/ppermute | solution.py:25
  221.0 38.4 %collective-permute-start.29 = (bf16[2,2,2,64,2048]{4,3,2,0,1:T(8,128)(2,1)}, bf16[2,2,2,64,2048]{4,3,2,0,1:T(8,128)(2,1)}, u32[]{:S(2)}, u32[]{:S(2)}) collective-permute-start(bf16[2,2,2,64,2048]{4,3,2,0,1:T(8,128)(2,1)} %bitcast.258), channel_id=1, source_target_pairs={{0,2},{2,0},{4,6},{6,4},{8,10},{10,8},{12,14},{14,12},{16,18},{18,... | collective-permute-start | bytes 6291464 | tf_op jit(solution)/shard_map/ppermute | solution.py:25
  253.6 24.5 %collective-permute-start.6 = (bf16[512,1024]{1,0:T(8,128)(2,1)}, bf16[512,1024]{1,0:T(8,128)(2,1)S(1)}, u32[]{:S(2)}, u32[]{:S(2)}) collective-permute-start(bf16[512,1024]{1,0:T(8,128)(2,1)} %get-tuple-element.174), channel_id=1, source_target_pairs={{0,1},{1,0},{2,3},{3,2},{4,5},{5,4},{6,7},{7,6},{8,9},{9,8},{10,11... | collective-permute-start | bytes 3145736 | tf_op jit(solution)/shard_map/ppermute | solution.py:25
  259.2 146.3 %collective-permute-start.26 = (bf16[2,2,64,2048]{3,2,0,1:T(8,128)(2,1)}, bf16[2,2,64,2048]{3,2,0,1:T(8,128)(2,1)}, u32[]{:S(2)}, u32[]{:S(2)}) collective-permute-start(bf16[2,2,64,2048]{3,2,0,1:T(8,128)(2,1)} %dynamic-slice_bitcast_fusion.1), channel_id=1, source_target_pairs={{0,4},{2,6},{4,0},{6,2},{8,12},{10,14},{12,8},{14,10},{16,20},{18,... | collective-permute-start | bytes 3145736 | tf_op jit(solution)/shard_map/ppermute | solution.py:25
  263.4 149.4 %collective-permute-start.30 = (bf16[2,2,64,2048]{3,2,1,0:T(8,128)(2,1)}, bf16[2,2,64,2048]{3,2,1,0:T(8,128)(2,1)}, u32[]{:S(2)}, u32[]{:S(2)}) collective-permute-start(bf16[2,2,64,2048]{3,2,1,0:T(8,128)(2,1)} %dynamic-slice_bitcast_fusion), channel_id=1, source_target_pairs={{0,8},{2,10},{4,12},{6,14},{8,0},{10,2},{12,4},{14,6},{16,24},{18,... | collective-permute-start | bytes 3145736 | tf_op jit(solution)/shard_map/ppermute | solution.py:25
  300.2 56.6 %collective-permute-start.21 = (bf16[2,2,2,64,512]{4,3,2,0,1:T(8,128)(2,1)}, bf16[2,2,2,64,512]{4,3,2,0,1:T(8,128)(2,1)}, u32[]{:S(2)}, u32[]{:S(2)}) collective-permute-start(bf16[2,2,2,64,512]{4,3,2,0,1:T(8,128)(2,1)} %bitcast.262), channel_id=1, source_target_pairs={{0,2},{2,0},{4,6},{6,4},{8,10},{10,8},{12,14},{14,12},{16,18},{18,... | collective-permute-start | bytes 1572872 | tf_op jit(solution)/shard_map/ppermute | solution.py:25
  352.3 15.3 %collective-permute-start.13 = (bf16[2,2,2,64,768]{4,3,0,1,2:T(8,128)(2,1)S(1)}, bf16[2,2,2,64,768]{4,3,0,1,2:T(8,128)(2,1)S(1)}, u32[]{:S(2)}, u32[]{:S(2)}) collective-permute-start(bf16[2,2,2,64,768]{4,3,0,1,2:T(8,128)(2,1)S(1)} %bitcast.293), channel_id=1, source_target_pairs={{0,2},{2,0},{4,6},{6,4},{8,10},{10,8},{12,14},{14,12},{16,18},{18,... | collective-permute-start | bytes 2359304 | tf_op jit(solution)/shard_map/ppermute | solution.py:25
  352.9 17.7 %collective-permute-start.17 = (bf16[2,2,2,64,768]{4,3,2,0,1:T(8,128)(2,1)S(1)}, bf16[2,2,2,64,768]{4,3,2,0,1:T(8,128)(2,1)S(1)}, u32[]{:S(2)}, u32[]{:S(2)}) collective-permute-start(bf16[2,2,2,64,768]{4,3,2,0,1:T(8,128)(2,1)S(1)} %bitcast.292), channel_id=1, source_target_pairs={{0,2},{2,0},{4,6},{6,4},{8,10},{10,8},{12,14},{14,12},{16,18},{18,... | collective-permute-start | bytes 2359304 | tf_op jit(solution)/shard_map/ppermute | solution.py:25
  358.1 8.6 %collective-permute-start.22 = (bf16[2,2,64,512]{3,2,1,0:T(8,128)(2,1)S(1)}, bf16[2,2,64,512]{3,2,1,0:T(8,128)(2,1)S(1)}, u32[]{:S(2)}, u32[]{:S(2)}) collective-permute-start(bf16[2,2,64,512]{3,2,1,0:T(8,128)(2,1)S(1)} %dynamic-slice_bitcast_fusion.8), channel_id=1, source_target_pairs={{0,8},{2,10},{4,12},{6,14},{8,0},{10,2},{12,4},{14,6},{16,24},{18,... | collective-permute-start | bytes 786440 | tf_op jit(solution)/shard_map/ppermute | solution.py:25
  366.8 24.6 %collective-permute-start.7 = (bf16[512,1024]{1,0:T(8,128)(2,1)S(1)}, bf16[512,1024]{1,0:T(8,128)(2,1)S(1)}, u32[]{:S(2)}, u32[]{:S(2)}) collective-permute-start(bf16[512,1024]{1,0:T(8,128)(2,1)S(1)} %fusion.64), channel_id=1, source_target_pairs={{0,1},{1,0},{2,3},{3,2},{4,5},{5,4},{6,7},{7,6},{8,9},{9,8},{10,11... | collective-permute-start | bytes 3145736 | tf_op jit(solution)/shard_map/ppermute | solution.py:25
  367.6 8.4 %collective-permute-start.23 = (bf16[2,64,512]{2,1,0:T(8,128)(2,1)S(1)}, bf16[2,64,512]{2,1,0:T(8,128)(2,1)S(1)}, u32[]{:S(2)}, u32[]{:S(2)}) collective-permute-start(bf16[2,64,512]{2,1,0:T(8,128)(2,1)S(1)} %dynamic-slice_bitcast_fusion.11), channel_id=1, source_target_pairs={{0,16},{2,18},{4,20},{6,22},{8,24},{10,26},{12,28},{14,30},{16,0},... | collective-permute-start | bytes 393224 | tf_op jit(solution)/shard_map/ppermute | solution.py:25
  370.6 61.4 %collective-permute-start.14 = (bf16[2,2,64,768]{3,2,0,1:T(8,128)(2,1)}, bf16[2,2,64,768]{3,2,0,1:T(8,128)(2,1)}, u32[]{:S(2)}, u32[]{:S(2)}) collective-permute-start(bf16[2,2,64,768]{3,2,0,1:T(8,128)(2,1)} %dynamic-slice_bitcast_fusion.5), channel_id=1, source_target_pairs={{0,4},{2,6},{4,0},{6,2},{8,12},{10,14},{12,8},{14,10},{16,20},{18,... | collective-permute-start | bytes 1179656 | tf_op jit(solution)/shard_map/ppermute | solution.py:25
  376.1 58.6 %collective-permute-start.18 = (bf16[2,2,64,768]{3,2,1,0:T(8,128)(2,1)}, bf16[2,2,64,768]{3,2,1,0:T(8,128)(2,1)}, u32[]{:S(2)}, u32[]{:S(2)}) collective-permute-start(bf16[2,2,64,768]{3,2,1,0:T(8,128)(2,1)} %dynamic-slice_bitcast_fusion.4), channel_id=1, source_target_pairs={{0,8},{2,10},{4,12},{6,14},{8,0},{10,2},{12,4},{14,6},{16,24},{18,... | collective-permute-start | bytes 1179656 | tf_op jit(solution)/shard_map/ppermute | solution.py:25
  391.4 10.1 %collective-permute-start.24 = (bf16[64,512]{1,0:T(8,128)(2,1)}, bf16[64,512]{1,0:T(8,128)(2,1)}, u32[]{:S(2)}, u32[]{:S(2)}) collective-permute-start(bf16[64,512]{1,0:T(8,128)(2,1)} %dynamic-slice_bitcast_fusion.14), channel_id=1, source_target_pairs={{0,4},{2,6},{4,0},{6,2},{8,12},{10,14},{12,8},{14,10},{16,20},{18,... | collective-permute-start | bytes 196616 | tf_op jit(solution)/shard_map/ppermute | solution.py:25
  410.3 57.6 %collective-permute-start.27 = (bf16[2,64,2048]{2,1,0:T(8,128)(2,1)}, bf16[2,64,2048]{2,1,0:T(8,128)(2,1)}, u32[]{:S(2)}, u32[]{:S(2)}) collective-permute-start(bf16[2,64,2048]{2,1,0:T(8,128)(2,1)} %dynamic-slice_bitcast_fusion.3), channel_id=1, source_target_pairs={{0,8},{2,10},{4,12},{6,14},{8,0},{10,2},{12,4},{14,6},{16,24},{18,... | collective-permute-start | bytes 1572872 | tf_op jit(solution)/shard_map/ppermute | solution.py:25
  411.8 12.9 %collective-permute-start.11 = (f32[2,1,384]{2,1,0:T(1,128)S(1)}, f32[2,1,384]{2,1,0:T(1,128)S(1)}, u32[]{:S(2)}, u32[]{:S(2)}) collective-permute-start(f32[2,1,384]{2,1,0:T(1,128)S(1)} %fusion.124), channel_id=1, source_target_pairs={{0,8},{2,10},{4,12},{6,14},{8,0},{10,2},{12,4},{14,6},{16,24},{18,... | collective-permute-start | bytes 9224 | tf_op jit(solution)/shard_map/ppermute | solution.py:25
  424.7 4.8 collective-permute-start.12
  426.5 42.6 %collective-permute-start.31 = (bf16[2,64,2048]{2,1,0:T(8,128)(2,1)S(1)}, bf16[2,64,2048]{2,1,0:T(8,128)(2,1)S(1)}, u32[]{:S(2)}, u32[]{:S(2)}) collective-permute-start(bf16[2,64,2048]{2,1,0:T(8,128)(2,1)S(1)} %dynamic-slice_bitcast_fusion.2), channel_id=1, source_target_pairs={{0,16},{2,18},{4,20},{6,22},{8,24},{10,26},{12,28},{14,30},{16,0},... | collective-permute-start | bytes 1572872 | tf_op jit(solution)/shard_map/ppermute | solution.py:25
  433.3 11.1 %collective-permute-start.15 = (bf16[2,64,768]{2,1,0:T(8,128)(2,1)S(1)}, bf16[2,64,768]{2,1,0:T(8,128)(2,1)S(1)}, u32[]{:S(2)}, u32[]{:S(2)}) collective-permute-start(bf16[2,64,768]{2,1,0:T(8,128)(2,1)S(1)} %dynamic-slice_bitcast_fusion.10), channel_id=1, source_target_pairs={{0,8},{2,10},{4,12},{6,14},{8,0},{10,2},{12,4},{14,6},{16,24},{18,... | collective-permute-start | bytes 589832 | tf_op jit(solution)/shard_map/ppermute | solution.py:25
  435.9 26.3 %collective-permute-start.19 = (bf16[2,64,768]{2,1,0:T(8,128)(2,1)S(1)}, bf16[2,64,768]{2,1,0:T(8,128)(2,1)S(1)}, u32[]{:S(2)}, u32[]{:S(2)}) collective-permute-start(bf16[2,64,768]{2,1,0:T(8,128)(2,1)S(1)} %dynamic-slice_bitcast_fusion.9), channel_id=1, source_target_pairs={{0,16},{2,18},{4,20},{6,22},{8,24},{10,26},{12,28},{14,30},{16,0},... | collective-permute-start | bytes 589832 | tf_op jit(solution)/shard_map/ppermute | solution.py:25
  444.5 19.8 %collective-permute-start.16 = (bf16[64,768]{1,0:T(8,128)(2,1)S(1)}, bf16[64,768]{1,0:T(8,128)(2,1)S(1)}, u32[]{:S(2)}, u32[]{:S(2)}) collective-permute-start(bf16[64,768]{1,0:T(8,128)(2,1)S(1)} %dynamic-slice_bitcast_fusion.13), channel_id=1, source_target_pairs={{0,16},{2,18},{4,20},{6,22},{8,24},{10,26},{12,28},{14,30},{16,0},... | collective-permute-start | bytes 294920 | tf_op jit(solution)/shard_map/ppermute | solution.py:25
  462.3 4.7 collective-permute-start.20
  469.1 13.1 %collective-permute-start.28 = (bf16[64,2048]{1,0:T(8,128)(2,1)S(1)}, bf16[64,2048]{1,0:T(8,128)(2,1)S(1)}, u32[]{:S(2)}, u32[]{:S(2)}) collective-permute-start(bf16[64,2048]{1,0:T(8,128)(2,1)S(1)} %dynamic-slice_bitcast_fusion.7), channel_id=1, source_target_pairs={{0,16},{2,18},{4,20},{6,22},{8,24},{10,26},{12,28},{14,30},{16,0},... | collective-permute-start | bytes 786440 | tf_op jit(solution)/shard_map/ppermute | solution.py:25
  469.4 13.7 %collective-permute-start.32 = (bf16[64,2048]{1,0:T(8,128)(2,1)S(1)}, bf16[64,2048]{1,0:T(8,128)(2,1)S(1)}, u32[]{:S(2)}, u32[]{:S(2)}) collective-permute-start(bf16[64,2048]{1,0:T(8,128)(2,1)S(1)} %dynamic-slice_bitcast_fusion.6), channel_id=1, source_target_pairs={{0,4},{2,6},{4,0},{6,2},{8,12},{10,14},{12,8},{14,10},{16,20},{18,... | collective-permute-start | bytes 786440 | tf_op jit(solution)/shard_map/ppermute | solution.py:25
  (86 other events, 1051.3 us)
Sparse Core Ops, SparseCore 0:
  10.8 53.2 all-gather.2
  66.8 73.3 all-gather.4
where the time goes:
time: 494 us; the launch traced here: 491 us
  waiting for transfers between devices  210 us (43%)
  matrix products  125 us (25%)
  other arithmetic  59.5 us (12%)
  local copies, waits for them, and re-layouts  49.2 us (10%)
  starting transfers between devices  31.9 us (6%)
  between operations  15.6 us (3%)
    ppermute x33, waiting for transfers between devices, xor_send(): return lax.ppermute(value, axis, [(i, i ^ distance) for i in range(size)])  185 us
    ppermute x33, starting transfers between devices, xor_send(): return lax.ppermute(value, axis, [(i, i ^ distance) for i in range(size)])  31.8 us
    dot_general x8, matrix products, times_transposed(): lax.dot_general(rows, weight, (((1,), (1,)), ((), ())), preferred_element...  29 us
    all_gather x2, waiting for transfers between devices, join_shards(): lax.all_gather(jnp.concatenate(shards, axis=1), 'dp', axis=0, tiled=True)  24.3 us
    convert_element_type x15, other arithmetic, halving_sum(): value = value.astype(keep_dtype)  14.7 us
    unnamed x172, local copies, waits for them, and re-layouts  14.6 us
    convert_element_type x2, other arithmetic, one_seq(): dscores = (probs * (dprobs - inner)).astype(jnp.bfloat16)  14.5 us
    dot_general x1, matrix products, per_device(): jnp.dot(full_dy, down_turned, preferred_element_type=jnp.float32)  13.2 us
  transfers between devices with their start and end apart: 35, of which 18 were waited for; matrix products, arithmetic and copies ran while one was open for 41% of the time, Pallas kernels for 0%

commit v1 on v0

--- a/solution.py
+++ b/solution.py
@@ -27,7 +27,25 @@
 
 def join_shards(*shards):
     widths = [shard.shape[1] for shard in shards]
-    full = lax.all_gather(jnp.concatenate(shards, axis=1), "dp", axis=0, tiled=True)
+    x = jnp.concatenate(shards, axis=1)
+    peers, place_2, rows_2 = (lax.axis_size("dp"), lax.axis_index("dp"), x.shape[0])
+    ahead_2 = [(i_2, (i_2 + 1) % peers) for i_2 in range(peers)]
+    behind = [(i_2, (i_2 - 1) % peers) for i_2 in range(peers)]
+    out = jnp.zeros((*x.shape[:0], peers * rows_2, *x.shape[0 + 1 :]), x.dtype)
+    out = lax.dynamic_update_slice_in_dim(out, x, place_2 * rows_2, axis=0)
+    from_left = from_right = x
+    half_2 = peers // 2
+    for lap in range(1, half_2 + 1):
+        from_left = lax.ppermute(from_left, "dp", ahead_2)
+        out = lax.dynamic_update_slice_in_dim(
+            out, from_left, (place_2 - lap) % peers * rows_2, axis=0
+        )
+        if lap < peers - half_2:
+            from_right = lax.ppermute(from_right, "dp", behind)
+            out = lax.dynamic_update_slice_in_dim(
+                out, from_right, (place_2 + lap) % peers * rows_2, axis=0
+            )
+    full = out
     parts = []
     start = 0
     for width in widths:

time: 494 us -> 519 us (1.051)
  starting transfers between devices: 31.9 us -> 155 us
  waiting for transfers between devices: 210 us -> 103 us
  local copies, waits for them, and re-layouts: 49.2 us -> 76.4 us
  between operations: 15.6 us -> 2.56 us
  matrix products: 125 us -> 117 us
    ppermute x33, waiting for transfers between devices: 185 us -> 80.6 us  [xor_send(): return lax.ppermute(value, axis, [(i, i ^ distance) for i in range(size)])]
    ppermute x0 -> x30, starting transfers between devices: none -> 85.5 us  [the longest x16 56.9 us: join_shards(): from_left = lax.ppermute(from_left, 'dp', ahead_2)]
    ppermute x33, starting transfers between devices: 31.8 us -> 69.7 us  [xor_send(): return lax.ppermute(value, axis, [(i, i ^ distance) for i in range(size)])]
    dynamic_update_slice x0 -> x30, local copies, waits for them, and re-layouts: none -> 24.6 us  [the longest x16 12.8 us: join_shards(): lax.dynamic_update_slice_in_dim(out, from_left, (place_2 - lap) % peers *...]
    all_gather x2 -> x0, waiting for transfers between devices: 24.3 us -> none  [join_shards(): lax.all_gather(jnp.concatenate(shards, axis=1), 'dp', axis=0, tiled=True)]
    ppermute x0 -> x30, waiting for transfers between devices: none -> 22.8 us  [the longest x16 16.6 us: join_shards(): from_left = lax.ppermute(from_left, 'dp', ahead_2)]
    dot_general x8, matrix products: 29 us -> 23.5 us  [times_transposed(): lax.dot_general(rows, weight, (((1,), (1,)), ((), ())), preferred_element...]
    unnamed x172 -> x164, local copies, waits for them, and re-layouts: 14.6 us -> 11.3 us
  transfers between devices with their start and end apart: 35 -> 63, of which waited for: 18 -> 21; matrix products, arithmetic and copies ran while one was open for 41% -> 41% of each run, Pallas kernels for 0% -> 0%
where the time goes in v1:
time: 519 us; the launch traced here: 513 us
  starting transfers between devices  155 us (30%)
  matrix products  117 us (23%)
  waiting for transfers between devices  103 us (20%)
  local copies, waits for them, and re-layouts  76.4 us (15%)
  other arithmetic  58 us (11%)
    ppermute x33, waiting for transfers between devices, xor_send(): return lax.ppermute(value, axis, [(i, i ^ distance) for i in range(size)])  80.6 us
    ppermute x33, starting transfers between devices, xor_send(): return lax.ppermute(value, axis, [(i, i ^ distance) for i in range(size)])  69.7 us
    ppermute x16, starting transfers between devices, join_shards(): from_left = lax.ppermute(from_left, 'dp', ahead_2)  56.9 us
    ppermute x14, starting transfers between devices, join_shards(): from_right = lax.ppermute(from_right, 'dp', behind)  28.6 us
    dot_general x8, matrix products, times_transposed(): lax.dot_general(rows, weight, (((1,), (1,)), ((), ())), preferred_element...  23.5 us
    ppermute x16, waiting for transfers between devices, join_shards(): from_left = lax.ppermute(from_left, 'dp', ahead_2)  16.6 us
    convert_element_type x2, other arithmetic, one_seq(): dscores = (probs * (dprobs - inner)).astype(jnp.bfloat16)  14.6 us
    convert_element_type x15, other arithmetic, halving_sum(): value = value.astype(keep_dtype)  14.1 us
  transfers between devices with their start and end apart: 63, of which 21 were waited for; matrix products, arithmetic and copies ran while one was open for 41% of the time, Pallas kernels for 0%

profile of v1, /device:TPU:0, one launch (start us, length us, event | category | flops | bytes accessed | tf_op | source)
XLA Modules:
  0.0 512.8 jit_solution(18029083934143751777)
XLA Ops:
  3.4 5.0 collective-permute-start.2
  42.8 5.0 collective-permute-done.5
  85.7 7.2 %collective-permute-start.13 = (bf16[64,2048]{1,0:T(8,128)(2,1)S(1)}, bf16[64,2048]{1,0:T(8,128)(2,1)S(1)}, u32[]{:S(2)}, u32[]{:S(2)}) collective-permute-start(bf16[64,2048]{1,0:T(8,128)(2,1)S(1)} %collective-permute-done.11), channel_id=1, source_target_pairs={{0,2},{2,4},{4,6},{6,8},{8,10},{10,12},{12,14},{14,16},{16,18},{18... | collective-permute-start | bytes 786440 | tf_op jit(solution)/shard_map/ppermute | solution.py:39
  94.3 10.1 %collective-permute-start.15 = (bf16[64,2048]{1,0:T(8,128)(2,1)S(1)}, bf16[64,2048]{1,0:T(8,128)(2,1)S(1)}, u32[]{:S(2)}, u32[]{:S(2)}) collective-permute-start(bf16[64,2048]{1,0:T(8,128)(2,1)S(1)} %collective-permute-done.13), channel_id=1, source_target_pairs={{0,2},{2,4},{4,6},{6,8},{8,10},{10,12},{12,14},{14,16},{16,18},{18... | collective-permute-start | bytes 786440 | tf_op jit(solution)/shard_map/ppermute | solution.py:39
  107.6 6.3 %add_convert_fusion = bf16[1024,1536]{1,0:T(8,128)(2,1)S(1)} fusion(f32[1536]{0:T(1024)S(1)} %pad_maximum_fusion.17, bf16[1024,2048]{1,0:T(8,128)(2,1)} %constant_dynamic-update-slice_fusion.16, bf16[512,1024]{1,0:T(8,128)(2,1)S(1)} %collective-permute-done, bf16[512,1024]{1,0:T(8,128)(2,1)S(1)} %fusion.46), kind=kOutput, calls=%fused_computation.32 | convolution fusion | flops 3228565504 | bytes 8394752 | tf_op jit(solution)/shard_map/dot_general | solution.py:238
  122.6 5.8 %fusion.152 = (f32[8,512]{1,0:T(8,128)S(1)}, f32[8,512,1024]{2,1,0:T(8,128)S(1)}) fusion(bf16[1,1024,3,8,64]{1,4,3,2,0:T(8,128)(2,1)} %bitcast.269, pred[512,1024]{1,0:T(8,128)(4,1)S(1)} %copy-done.28), kind=kOutput, calls=%fused_computation.322 | convolution fusion | flops 549449728 | bytes 18890752 | tf_op jit(solution)/shard_map/while/body/eval_jaxpr/qhd,khd->hqk/dot_general | solution.py:152
  134.2 5.3 %fusion.95 = bf16[8,64,512]{2,1,0:T(8,128)(2,1)} fusion(f32[8,512,1024]{2,1,0:T(8,128)S(1)} %get-tuple-element.221, f32[8,512]{1,0:T(8,128)S(1)} %fusion, f32[8,512]{1,0:T(8,128)S(1)} %get-tuple-element.220, bf16[1,1024,3,8,64]{1,4,3,2,0:T(8,128)(2,1)} %bitcast.270), kind=kOutput, calls=%fused_computation.135 | convolution fusion | flops 549715968 | bytes 18382848 | tf_op jit(solution)/shard_map/while/body/eval_jaxpr/hqk,khd->qhd/dot_general | solution.py:166
  157.4 7.4 %collective-permute-start.28 = (bf16[64,4096]{1,0:T(8,128)(2,1)S(1)}, bf16[64,4096]{1,0:T(8,128)(2,1)S(1)}, u32[]{:S(2)}, u32[]{:S(2)}) collective-permute-start(bf16[64,4096]{1,0:T(8,128)(2,1)S(1)} %collective-permute-done.26), channel_id=1, source_target_pairs={{0,2},{2,4},{4,6},{6,8},{8,10},{10,12},{12,14},{14,16},{16,18},{18... | collective-permute-start | bytes 1572872 | tf_op jit(solution)/shard_map/ppermute | solution.py:39
  170.4 8.6 %collective-permute-start.30 = (bf16[64,4096]{1,0:T(8,128)(2,1)S(1)}, bf16[64,4096]{1,0:T(8,128)(2,1)S(1)}, u32[]{:S(2)}, u32[]{:S(2)}) collective-permute-start(bf16[64,4096]{1,0:T(8,128)(2,1)S(1)} %collective-permute-done.28), channel_id=1, source_target_pairs={{0,2},{2,4},{4,6},{6,8},{8,10},{10,12},{12,14},{14,16},{16,18},{18... | collective-permute-start | bytes 1572872 | tf_op jit(solution)/shard_map/ppermute | solution.py:39
  181.7 11.7 %collective-permute-start.32 = (bf16[64,4096]{1,0:T(8,128)(2,1)S(1)}, bf16[64,4096]{1,0:T(8,128)(2,1)S(1)}, u32[]{:S(2)}, u32[]{:S(2)}) collective-permute-start(bf16[64,4096]{1,0:T(8,128)(2,1)S(1)} %collective-permute-done.30), channel_id=1, source_target_pairs={{0,2},{2,4},{4,6},{6,8},{8,10},{10,12},{12,14},{14,16},{16,18},{18... | collective-permute-start | bytes 1572872 | tf_op jit(solution)/shard_map/ppermute | solution.py:39
  195.0 6.1 %multiply_convert_fusion.2 = (bf16[1024,2048]{1,0:T(8,128)(2,1)S(1)}, f32[1024,2048]{1,0:T(8,128)S(1)}) fusion(f32[2048]{0:T(1024)S(1)} %copy-done.62, bf16[1024,4096]{1,0:T(8,128)(2,1)S(1)} %constant_dynamic-update-slice_fusion, bf16[512,1024]{1,0:T(8,128)(2,1)S(1)} %collective-permute-done.17, bf16[512,1024]{1,0:T(8,128)(2,1)S(1)} %add_convert_fusion.3), kind=kOutput, calls=%fused_computation.24 | convolution fusion | flops 4320133120 | bytes 18882560 | tf_op jit(solution)/shard_map/dot_general | solution.py:249
  204.5 6.5 %convolution_convert_fusion.1 = bf16[1024,2048]{1,0:T(8,128)(2,1)} fusion(bf16[1024,1024]{1,0:T(8,128)(2,1)S(1)} %copy-done.35, bf16[1024,2048]{1,0:T(8,128)(2,1)S(1)} %get-tuple-element.224), kind=kOutput, calls=%fused_computation.41 | convolution fusion | flops 4297064448 | bytes 10485760 | tf_op jit(solution)/shard_map/dot_general | solution.py:258
  210.9 11.4 %convert_reduce_fusion = (f32[2048]{0:T(1024)S(1)}, bf16[1024,2048]{1,0:T(8,128)(2,1)S(1)}) fusion(bf16[1024,1024]{1,0:T(8,128)(2,1)S(1)} %copy-done.35, bf16[1024,4096]{1,0:T(8,128)(2,1)S(1)} %constant_dynamic-update-slice_fusion, f32[1024,2048]{1,0:T(8,128)S(1)} %get-tuple-element.225, f32[2048]{0:T(1024)S(1)} %copy-done.62), kind=kOutput, calls=%fused_computation.19 | convolution fusion | flops 4351588352 | bytes 18890752 | tf_op jit(solution)/shard_map/dot_general | solution.py:248
  226.9 6.7 %convolution_convert_fusion.2 = bf16[1024,2048]{1,0:T(8,128)(2,1)} fusion(bf16[1024,2048]{1,0:T(8,128)(2,1)S(1)} %get-tuple-element.233, bf16[512,1024]{1,0:T(8,128)(2,1)S(1)} %collective-permute-done.17, bf16[512,1024]{1,0:T(8,128)(2,1)S(1)} %add_convert_fusion.3), kind=kOutput, calls=%fused_computation.42 | convolution fusion | flops 4301258752 | bytes 10485760 | tf_op jit(solution)/shard_map/dot_general | solution.py:261
  233.6 6.7 %constant_dynamic-slice_fusion.1 = (bf16[2,2,2,1,64,2048]{5,4,3,2,1,0:T(8,128)(2,1)}, bf16[2,2,2,1,64,2048]{5,4,3,2,1,0:T(8,128)(2,1)S(1)}, bf16[2,2,2,1,64,2048...) fusion(bf16[2,2,2,2,64,2048]{5,4,3,2,1,0:T(8,128)(2,1)} %bitcast.288, s32[]{:T(128)S(6)} %select_n.395, ...), kind=kLoop, calls=%fused_computation.216 | loop fusion | bytes 16777224 | tf_op jit(solution)/shard_map/jit(dynamic_index_in_dim)/dynamic_slice | solution.py:113
  243.1 6.5 %collective-permute-start.55 = (bf16[2,2,2,64,2048]{4,3,0,1,2:T(8,128)(2,1)}, bf16[2,2,2,64,2048]{4,3,0,1,2:T(8,128)(2,1)}, u32[]{:S(2)}, u32[]{:S(2)}) collective-permute-start(bf16[2,2,2,64,2048]{4,3,0,1,2:T(8,128)(2,1)} %bitcast.259), channel_id=1, source_target_pairs={{0,2},{2,0},{4,6},{6,4},{8,10},{10,8},{12,14},{14,12},{16,18},{18,... | collective-permute-start | bytes 6291464 | tf_op jit(solution)/shard_map/ppermute | solution.py:25
  249.6 17.7 %collective-permute-done.35 = bf16[512,1024]{1,0:T(8,128)(2,1)S(1)} collective-permute-done((bf16[512,1024]{1,0:T(8,128)(2,1)S(1)}, bf16[512,1024]{1,0:T(8,128)(2,1)S(1)}, u32[]{:S(2)}, u32[]{:S(2)}) %collective-permute-start.35) | collective-permute-done | bytes 1048608 | tf_op jit(solution)/shard_map/ppermute | solution.py:25
  277.8 6.6 %add_convert_fusion.2 = bf16[512,1024]{1,0:T(8,128)(2,1)} fusion(f32[512,1024]{1,0:T(8,128)S(1)} %get-tuple-element.223, bf16[512,1024]{1,0:T(8,128)(2,1)} %collective-permute-done.33, bf16[1024,4096]{1,0:T(8,128)(2,1)} %copy-done.16, bf16[1024,2048]{1,0:T(8,128)(2,1)} %copy-done.67, f32[1024]{0:T(1024)S(1)} %bitcast.317), kind=kOutput, calls=%fused_computation.107 | convolution fusion | flops 2150105088 | bytes 10489856 | tf_op jit(solution)/shard_map/dot_general | solution.py:97
  288.1 8.0 %collective-permute-start.56 = (bf16[2,2,64,2048]{3,2,0,1:T(8,128)(2,1)}, bf16[2,2,64,2048]{3,2,0,1:T(8,128)(2,1)}, u32[]{:S(2)}, u32[]{:S(2)}) collective-permute-start(bf16[2,2,64,2048]{3,2,0,1:T(8,128)(2,1)} %dynamic-slice_bitcast_fusion.1), channel_id=1, source_target_pairs={{0,4},{2,6},{4,0},{6,2},{8,12},{10,14},{12,8},{14,10},{16,20},{18,... | collective-permute-start | bytes 3145736 | tf_op jit(solution)/shard_map/ppermute | solution.py:25
  299.8 4.9 collective-permute-start.60
  326.0 10.0 %multiply_reduce_fusion = (f32[8,512]{1,0:T(8,128)}, f32[8,512,1024]{2,1,0:T(8,128)}) fusion(f32[8,512,1024]{2,1,0:T(8,128)S(1)} %bitcast.265, f32[8,512]{1,0:T(8,128)} %log_add_fusion, bf16[512,8,64]{0,2,1:T(8,128)(2,1)} %bitcast.283, bf16[1,1024,3,8,64]{1,4,3,2,0:T(8,128)(2,1)} %bitcast.275), kind=kOutput, calls=%fused_computation.1 | convolution fusion | flops 549449728 | bytes 35160064 | tf_op jit(solution)/shard_map/while/body/eval_jaxpr/qhd,khd->hqk/dot_general | solution.py:197
  336.0 5.0 fusion.57
  344.5 12.0 %multiply_convert_fusion = bf16[8,512,1024]{2,1,0:T(8,128)(2,1)S(1)} fusion(f32[8,512,1024]{2,1,0:T(8,128)} %get-tuple-element.230, f32[8,512,1024]{2,1,0:T(8,128)} %copy-done, f32[8,512]{1,0:T(8,128)} %get-tuple-element.229, f32[8,512]{1,0:T(8,128)} %log_add_fusion), kind=kLoop, calls=%fused_computation | loop fusion | flops 16777216 | bytes 41975808 | tf_op jit(solution)/shard_map/while/body/eval_jaxpr/convert_element_type | solution.py:201
  369.3 5.5 %convolution_convert_fusion = bf16[1024,1536]{1,0:T(8,128)(2,1)S(1)} fusion(bf16[512,1536]{1,0:T(8,128)(2,1)} %copy-done.17, bf16[512,1536]{1,0:T(8,128)(2,1)S(1)} %get-tuple-element.184, bf16[512,1024]{1,0:T(8,128)(2,1)} %copy-done.59, bf16[512,1024]{1,0:T(8,128)(2,1)} %copy-done.32), kind=kOutput, calls=%fused_computation.40 | convolution fusion | flops 3233284096 | bytes 8388608 | tf_op jit(solution)/shard_map/dot_general | solution.py:295
  388.8 5.9 %collective-permute-done.52 = bf16[2,2,64,512]{3,2,1,0:T(8,128)(2,1)S(1)} collective-permute-done((bf16[2,2,64,512]{3,2,1,0:T(8,128)(2,1)S(1)}, bf16[2,2,64,512]{3,2,1,0:T(8,128)(2,1)S(1)}, u32[]{:S(2)}, u32[]{:S(2)}) %collective-permute-start.52) | collective-permute-done | bytes 262176 | tf_op jit(solution)/shard_map/ppermute | solution.py:25
  395.3 6.4 %collective-permute-start.53 = (bf16[2,64,512]{2,1,0:T(8,128)(2,1)S(1)}, bf16[2,64,512]{2,1,0:T(8,128)(2,1)S(1)}, u32[]{:S(2)}, u32[]{:S(2)}) collective-permute-start(bf16[2,64,512]{2,1,0:T(8,128)(2,1)S(1)} %dynamic-slice_bitcast_fusion.11), channel_id=1, source_target_pairs={{0,16},{2,18},{4,20},{6,22},{8,24},{10,26},{12,28},{14,30},{16,0},... | collective-permute-start | bytes 393224 | tf_op jit(solution)/shard_map/ppermute | solution.py:25
  409.1 10.3 %collective-permute-done.37 = bf16[512,1024]{1,0:T(8,128)(2,1)S(1)} collective-permute-done((bf16[512,1024]{1,0:T(8,128)(2,1)S(1)}, bf16[512,1024]{1,0:T(8,128)(2,1)S(1)}, u32[]{:S(2)}, u32[]{:S(2)}) %collective-permute-start.37) | collective-permute-done | bytes 1048608 | tf_op jit(solution)/shard_map/ppermute | solution.py:25
  438.9 10.4 %collective-permute-done.41 = f32[2,1,384]{2,1,0:T(1,128)S(1)} collective-permute-done((f32[2,1,384]{2,1,0:T(1,128)S(1)}, f32[2,1,384]{2,1,0:T(1,128)S(1)}, u32[]{:S(2)}, u32[]{:S(2)}) %collective-permute-start.41) | collective-permute-done | bytes 3104 | tf_op jit(solution)/shard_map/ppermute | solution.py:25
  449.4 6.7 %collective-permute-start.42 = (f32[1,384]{1,0:T(1,128)S(1)}, f32[1,384]{1,0:T(1,128)S(1)}, u32[]{:S(2)}, u32[]{:S(2)}) collective-permute-start(f32[1,384]{1,0:T(1,128)S(1)} %fusion.134), channel_id=1, source_target_pairs={{0,16},{2,18},{4,20},{6,22},{8,24},{10,26},{12,28},{14,30},{16,0},... | collective-permute-start | bytes 4616 | tf_op jit(solution)/shard_map/ppermute | solution.py:25
  464.2 11.5 %collective-permute-start.49 = (bf16[2,64,768]{2,1,0:T(8,128)(2,1)S(1)}, bf16[2,64,768]{2,1,0:T(8,128)(2,1)S(1)}, u32[]{:S(2)}, u32[]{:S(2)}) collective-permute-start(bf16[2,64,768]{2,1,0:T(8,128)(2,1)S(1)} %dynamic-slice_bitcast_fusion.9), channel_id=1, source_target_pairs={{0,16},{2,18},{4,20},{6,22},{8,24},{10,26},{12,28},{14,30},{16,0},... | collective-permute-start | bytes 589832 | tf_op jit(solution)/shard_map/ppermute | solution.py:25
  480.1 12.8 %collective-permute-done.49 = bf16[2,64,768]{2,1,0:T(8,128)(2,1)S(1)} collective-permute-done((bf16[2,64,768]{2,1,0:T(8,128)(2,1)S(1)}, bf16[2,64,768]{2,1,0:T(8,128)(2,1)S(1)}, u32[]{:S(2)}, u32[]{:S(2)}) %collective-permute-start.49) | collective-permute-done | bytes 196640 | tf_op jit(solution)/shard_map/ppermute | solution.py:25
  500.6 10.2 %collective-permute-done.58 = bf16[64,2048]{1,0:T(8,128)(2,1)S(1)} collective-permute-done((bf16[64,2048]{1,0:T(8,128)(2,1)S(1)}, bf16[64,2048]{1,0:T(8,128)(2,1)S(1)}, u32[]{:S(2)}, u32[]{:S(2)}) %collective-permute-start.58) | collective-permute-done | bytes 262176 | tf_op jit(solution)/shard_map/ppermute | solution.py:25
  (448 shorter events, 250.0 us)
Async XLA Ops:
  2.9 19.2 %collective-permute-start.1 = (bf16[64,2048]{1,0:T(8,128)(2,1)}, bf16[64,2048]{1,0:T(8,128)(2,1)}, u32[]{:S(2)}, u32[]{:S(2)}) collective-permute-start(bf16[64,2048]{1,0:T(8,128)(2,1)} %get-tuple-element.202), channel_id=1, source_target_pairs={{0,2},{2,4},{4,6},{6,8},{8,10},{10,12},{12,14},{14,16},{16,18},{18... | collective-permute-start | bytes 786440 | tf_op jit(solution)/shard_map/ppermute | solution.py:39
  3.4 21.1 %collective-permute-start.2 = (bf16[64,2048]{1,0:T(8,128)(2,1)}, bf16[64,2048]{1,0:T(8,128)(2,1)}, u32[]{:S(2)}, u32[]{:S(2)}) collective-permute-start(bf16[64,2048]{1,0:T(8,128)(2,1)} %get-tuple-element.202), channel_id=1, source_target_pairs={{0,30},{2,0},{4,2},{6,4},{8,6},{10,8},{12,10},{14,12},{16,14},{18,... | collective-permute-start | bytes 786440 | tf_op jit(solution)/shard_map/ppermute | solution.py:44
  10.4 15.8 %collective-permute-start.18 = (bf16[64,4096]{1,0:T(8,128)(2,1)}, bf16[64,4096]{1,0:T(8,128)(2,1)}, u32[]{:S(2)}, u32[]{:S(2)}) collective-permute-start(bf16[64,4096]{1,0:T(8,128)(2,1)} %get-tuple-element.200), channel_id=1, source_target_pairs={{0,2},{2,4},{4,6},{6,8},{8,10},{10,12},{12,14},{14,16},{16,18},{18... | collective-permute-start | bytes 1572872 | tf_op jit(solution)/shard_map/ppermute | solution.py:39
  13.6 21.2 %collective-permute-start.19 = (bf16[64,4096]{1,0:T(8,128)(2,1)}, bf16[64,4096]{1,0:T(8,128)(2,1)}, u32[]{:S(2)}, u32[]{:S(2)}) collective-permute-start(bf16[64,4096]{1,0:T(8,128)(2,1)} %get-tuple-element.200), channel_id=1, source_target_pairs={{0,30},{2,0},{4,2},{6,4},{8,6},{10,8},{12,10},{14,12},{16,14},{18,... | collective-permute-start | bytes 1572872 | tf_op jit(solution)/shard_map/ppermute | solution.py:44
  15.6 53.3 %collective-permute-start.34 = (bf16[512,1024]{1,0:T(8,128)(2,1)S(1)}, bf16[512,1024]{1,0:T(8,128)(2,1)}, u32[]{:S(2)}, u32[]{:S(2)}) collective-permute-start(bf16[512,1024]{1,0:T(8,128)(2,1)S(1)} %copy-done.8), channel_id=1, source_target_pairs={{0,1},{1,0},{2,3},{3,2},{4,5},{5,4},{6,7},{7,6},{8,9},{9,8},{10,11... | collective-permute-start | bytes 3145736 | tf_op jit(solution)/shard_map/ppermute | solution.py:25
  22.2 84.5 %collective-permute-start = (bf16[512,1024]{1,0:T(8,128)(2,1)S(1)}, bf16[512,1024]{1,0:T(8,128)(2,1)S(1)}, u32[]{:S(2)}, u32[]{:S(2)}) collective-permute-start(bf16[512,1024]{1,0:T(8,128)(2,1)S(1)} %fusion.46), channel_id=1, source_target_pairs={{0,1},{1,0},{2,3},{3,2},{4,5},{5,4},{6,7},{7,6},{8,9},{9,8},{10,11... | collective-permute-start | bytes 3145736 | tf_op jit(solution)/shard_map/ppermute | solution.py:25
  33.3 23.0 %collective-permute-start.20 = (bf16[64,4096]{1,0:T(8,128)(2,1)}, bf16[64,4096]{1,0:T(8,128)(2,1)S(1)}, u32[]{:S(2)}, u32[]{:S(2)}) collective-permute-start(bf16[64,4096]{1,0:T(8,128)(2,1)} %collective-permute-done.18), channel_id=1, source_target_pairs={{0,2},{2,4},{4,6},{6,8},{8,10},{10,12},{12,14},{14,16},{16,18},{18... | collective-permute-start | bytes 1572872 | tf_op jit(solution)/shard_map/ppermute | solution.py:39
  48.5 17.3 %collective-permute-start.21 = (bf16[64,4096]{1,0:T(8,128)(2,1)}, bf16[64,4096]{1,0:T(8,128)(2,1)S(1)}, u32[]{:S(2)}, u32[]{:S(2)}) collective-permute-start(bf16[64,4096]{1,0:T(8,128)(2,1)} %collective-permute-done.19), channel_id=1, source_target_pairs={{0,30},{2,0},{4,2},{6,4},{8,6},{10,8},{12,10},{14,12},{16,14},{18,... | collective-permute-start | bytes 1572872 | tf_op jit(solution)/shard_map/ppermute | solution.py:44
  62.6 14.7 %collective-permute-start.22 = (bf16[64,4096]{1,0:T(8,128)(2,1)S(1)}, bf16[64,4096]{1,0:T(8,128)(2,1)}, u32[]{:S(2)}, u32[]{:S(2)}) collective-permute-start(bf16[64,4096]{1,0:T(8,128)(2,1)S(1)} %collective-permute-done.20), channel_id=1, source_target_pairs={{0,2},{2,4},{4,6},{6,8},{8,10},{10,12},{12,14},{14,16},{16,18},{18... | collective-permute-start | bytes 1572872 | tf_op jit(solution)/shard_map/ppermute | solution.py:39
  70.8 14.9 %collective-permute-start.11 = (bf16[64,2048]{1,0:T(8,128)(2,1)S(1)}, bf16[64,2048]{1,0:T(8,128)(2,1)S(1)}, u32[]{:S(2)}, u32[]{:S(2)}) collective-permute-start(bf16[64,2048]{1,0:T(8,128)(2,1)S(1)} %collective-permute-done.9), channel_id=1, source_target_pairs={{0,2},{2,4},{4,6},{6,8},{8,10},{10,12},{12,14},{14,16},{16,18},{18... | collective-permute-start | bytes 786440 | tf_op jit(solution)/shard_map/ppermute | solution.py:39
  71.3 21.6 %collective-permute-start.12 = (bf16[64,2048]{1,0:T(8,128)(2,1)S(1)}, bf16[64,2048]{1,0:T(8,128)(2,1)S(1)}, u32[]{:S(2)}, u32[]{:S(2)}) collective-permute-start(bf16[64,2048]{1,0:T(8,128)(2,1)S(1)} %collective-permute-done.10), channel_id=1, source_target_pairs={{0,30},{2,0},{4,2},{6,4},{8,6},{10,8},{12,10},{14,12},{16,14},{18,... | collective-permute-start | bytes 786440 | tf_op jit(solution)/shard_map/ppermute | solution.py:44
  77.4 68.5 %collective-permute-start.24 = (bf16[64,4096]{1,0:T(8,128)(2,1)}, bf16[64,4096]{1,0:T(8,128)(2,1)}, u32[]{:S(2)}, u32[]{:S(2)}) collective-permute-start(bf16[64,4096]{1,0:T(8,128)(2,1)} %collective-permute-done.22), channel_id=1, source_target_pairs={{0,2},{2,4},{4,6},{6,8},{8,10},{10,12},{12,14},{14,16},{16,18},{18... | collective-permute-start | bytes 1572872 | tf_op jit(solution)/shard_map/ppermute | solution.py:39
  83.0 68.1 %collective-permute-start.25 = (bf16[64,4096]{1,0:T(8,128)(2,1)}, bf16[64,4096]{1,0:T(8,128)(2,1)}, u32[]{:S(2)}, u32[]{:S(2)}) collective-permute-start(bf16[64,4096]{1,0:T(8,128)(2,1)} %collective-permute-done.23), channel_id=1, source_target_pairs={{0,30},{2,0},{4,2},{6,4},{8,6},{10,8},{12,10},{14,12},{16,14},{18,... | collective-permute-start | bytes 1572872 | tf_op jit(solution)/shard_map/ppermute | solution.py:44
  144.3 22.6 %collective-permute-start.16 = (bf16[512,1024]{1,0:T(8,128)(2,1)S(1)}, bf16[512,1024]{1,0:T(8,128)(2,1)S(1)}, u32[]{:S(2)}, u32[]{:S(2)}) collective-permute-start(bf16[512,1024]{1,0:T(8,128)(2,1)S(1)} %convolution_convert_fusion.5), channel_id=1, source_target_pairs={{0,1},{1,0},{2,3},{3,2},{4,5},{5,4},{6,7},{7,6},{8,9},{9,8},{10,11... | collective-permute-start | bytes 3145736 | tf_op jit(solution)/shard_map/ppermute | solution.py:25
  168.8 26.2 %collective-permute-start.17 = (bf16[512,1024]{1,0:T(8,128)(2,1)S(1)}, bf16[512,1024]{1,0:T(8,128)(2,1)S(1)}, u32[]{:S(2)}, u32[]{:S(2)}) collective-permute-start(bf16[512,1024]{1,0:T(8,128)(2,1)S(1)} %add_convert_fusion.3), channel_id=1, source_target_pairs={{0,1},{1,0},{2,3},{3,2},{4,5},{5,4},{6,7},{7,6},{8,9},{9,8},{10,11... | collective-permute-start | bytes 3145736 | tf_op jit(solution)/shard_map/ppermute | solution.py:25
  224.8 53.0 %collective-permute-start.33 = (bf16[512,1024]{1,0:T(8,128)(2,1)}, bf16[512,1024]{1,0:T(8,128)(2,1)}, u32[]{:S(2)}, u32[]{:S(2)}) collective-permute-start(bf16[512,1024]{1,0:T(8,128)(2,1)} %fusion.82), channel_id=1, source_target_pairs={{0,1},{1,0},{2,3},{3,2},{4,5},{5,4},{6,7},{7,6},{8,9},{9,8},{10,11... | collective-permute-start | bytes 3145736 | tf_op jit(solution)/shard_map/ppermute | solution.py:25
  225.3 42.1 %collective-permute-start.35 = (bf16[512,1024]{1,0:T(8,128)(2,1)S(1)}, bf16[512,1024]{1,0:T(8,128)(2,1)S(1)}, u32[]{:S(2)}, u32[]{:S(2)}) collective-permute-start(bf16[512,1024]{1,0:T(8,128)(2,1)S(1)} %fusion.77), channel_id=1, source_target_pairs={{0,1},{1,0},{2,3},{3,2},{4,5},{5,4},{6,7},{7,6},{8,9},{9,8},{10,11... | collective-permute-start | bytes 3145736 | tf_op jit(solution)/shard_map/ppermute | solution.py:25
  243.1 41.3 %collective-permute-start.55 = (bf16[2,2,2,64,2048]{4,3,0,1,2:T(8,128)(2,1)}, bf16[2,2,2,64,2048]{4,3,0,1,2:T(8,128)(2,1)}, u32[]{:S(2)}, u32[]{:S(2)}) collective-permute-start(bf16[2,2,2,64,2048]{4,3,0,1,2:T(8,128)(2,1)} %bitcast.259), channel_id=1, source_target_pairs={{0,2},{2,0},{4,6},{6,4},{8,10},{10,8},{12,14},{14,12},{16,18},{18,... | collective-permute-start | bytes 6291464 | tf_op jit(solution)/shard_map/ppermute | solution.py:25
  249.6 46.5 %collective-permute-start.59 = (bf16[2,2,2,64,2048]{4,3,2,0,1:T(8,128)(2,1)}, bf16[2,2,2,64,2048]{4,3,2,0,1:T(8,128)(2,1)}, u32[]{:S(2)}, u32[]{:S(2)}) collective-permute-start(bf16[2,2,2,64,2048]{4,3,2,0,1:T(8,128)(2,1)} %bitcast.258), channel_id=1, source_target_pairs={{0,2},{2,0},{4,6},{6,4},{8,10},{10,8},{12,14},{14,12},{16,18},{18,... | collective-permute-start | bytes 6291464 | tf_op jit(solution)/shard_map/ppermute | solution.py:25
  277.3 27.4 %collective-permute-start.36 = (bf16[512,1024]{1,0:T(8,128)(2,1)}, bf16[512,1024]{1,0:T(8,128)(2,1)S(1)}, u32[]{:S(2)}, u32[]{:S(2)}) collective-permute-start(bf16[512,1024]{1,0:T(8,128)(2,1)} %get-tuple-element.175), channel_id=1, source_target_pairs={{0,1},{1,0},{2,3},{3,2},{4,5},{5,4},{6,7},{7,6},{8,9},{9,8},{10,11... | collective-permute-start | bytes 3145736 | tf_op jit(solution)/shard_map/ppermute | solution.py:25
  288.1 142.0 %collective-permute-start.56 = (bf16[2,2,64,2048]{3,2,0,1:T(8,128)(2,1)}, bf16[2,2,64,2048]{3,2,0,1:T(8,128)(2,1)}, u32[]{:S(2)}, u32[]{:S(2)}) collective-permute-start(bf16[2,2,64,2048]{3,2,0,1:T(8,128)(2,1)} %dynamic-slice_bitcast_fusion.1), channel_id=1, source_target_pairs={{0,4},{2,6},{4,0},{6,2},{8,12},{10,14},{12,8},{14,10},{16,20},{18,... | collective-permute-start | bytes 3145736 | tf_op jit(solution)/shard_map/ppermute | solution.py:25
  299.8 137.5 %collective-permute-start.60 = (bf16[2,2,64,2048]{3,2,1,0:T(8,128)(2,1)}, bf16[2,2,64,2048]{3,2,1,0:T(8,128)(2,1)}, u32[]{:S(2)}, u32[]{:S(2)}) collective-permute-start(bf16[2,2,64,2048]{3,2,1,0:T(8,128)(2,1)} %dynamic-slice_bitcast_fusion), channel_id=1, source_target_pairs={{0,8},{2,10},{4,12},{6,14},{8,0},{10,2},{12,4},{14,6},{16,24},{18,... | collective-permute-start | bytes 3145736 | tf_op jit(solution)/shard_map/ppermute | solution.py:25
  325.9 56.9 %collective-permute-start.51 = (bf16[2,2,2,64,512]{4,3,2,0,1:T(8,128)(2,1)}, bf16[2,2,2,64,512]{4,3,2,0,1:T(8,128)(2,1)}, u32[]{:S(2)}, u32[]{:S(2)}) collective-permute-start(bf16[2,2,2,64,512]{4,3,2,0,1:T(8,128)(2,1)} %bitcast.262), channel_id=1, source_target_pairs={{0,2},{2,0},{4,6},{6,4},{8,10},{10,8},{12,14},{14,12},{16,18},{18,... | collective-permute-start | bytes 1572872 | tf_op jit(solution)/shard_map/ppermute | solution.py:25
  377.9 17.4 %collective-permute-start.43 = (bf16[2,2,2,64,768]{4,3,0,1,2:T(8,128)(2,1)S(1)}, bf16[2,2,2,64,768]{4,3,0,1,2:T(8,128)(2,1)S(1)}, u32[]{:S(2)}, u32[]{:S(2)}) collective-permute-start(bf16[2,2,2,64,768]{4,3,0,1,2:T(8,128)(2,1)S(1)} %bitcast.295), channel_id=1, source_target_pairs={{0,2},{2,0},{4,6},{6,4},{8,10},{10,8},{12,14},{14,12},{16,18},{18,... | collective-permute-start | bytes 2359304 | tf_op jit(solution)/shard_map/ppermute | solution.py:25
  378.5 24.3 %collective-permute-start.47 = (bf16[2,2,2,64,768]{4,3,2,0,1:T(8,128)(2,1)S(1)}, bf16[2,2,2,64,768]{4,3,2,0,1:T(8,128)(2,1)S(1)}, u32[]{:S(2)}, u32[]{:S(2)}) collective-permute-start(bf16[2,2,2,64,768]{4,3,2,0,1:T(8,128)(2,1)S(1)} %bitcast.294), channel_id=1, source_target_pairs={{0,2},{2,0},{4,6},{6,4},{8,10},{10,8},{12,14},{14,12},{16,18},{18,... | collective-permute-start | bytes 2359304 | tf_op jit(solution)/shard_map/ppermute | solution.py:25
  394.7 24.7 %collective-permute-start.37 = (bf16[512,1024]{1,0:T(8,128)(2,1)S(1)}, bf16[512,1024]{1,0:T(8,128)(2,1)S(1)}, u32[]{:S(2)}, u32[]{:S(2)}) collective-permute-start(bf16[512,1024]{1,0:T(8,128)(2,1)S(1)} %fusion.74), channel_id=1, source_target_pairs={{0,1},{1,0},{2,3},{3,2},{4,5},{5,4},{6,7},{7,6},{8,9},{9,8},{10,11... | collective-permute-start | bytes 3145736 | tf_op jit(solution)/shard_map/ppermute | solution.py:25
  402.8 57.4 %collective-permute-start.44 = (bf16[2,2,64,768]{3,2,0,1:T(8,128)(2,1)}, bf16[2,2,64,768]{3,2,0,1:T(8,128)(2,1)}, u32[]{:S(2)}, u32[]{:S(2)}) collective-permute-start(bf16[2,2,64,768]{3,2,0,1:T(8,128)(2,1)} %dynamic-slice_bitcast_fusion.5), channel_id=1, source_target_pairs={{0,4},{2,6},{4,0},{6,2},{8,12},{10,14},{12,8},{14,10},{16,20},{18,... | collective-permute-start | bytes 1179656 | tf_op jit(solution)/shard_map/ppermute | solution.py:25
  407.8 55.2 %collective-permute-start.48 = (bf16[2,2,64,768]{3,2,1,0:T(8,128)(2,1)}, bf16[2,2,64,768]{3,2,1,0:T(8,128)(2,1)}, u32[]{:S(2)}, u32[]{:S(2)}) collective-permute-start(bf16[2,2,64,768]{3,2,1,0:T(8,128)(2,1)} %dynamic-slice_bitcast_fusion.4), channel_id=1, source_target_pairs={{0,8},{2,10},{4,12},{6,14},{8,0},{10,2},{12,4},{14,6},{16,24},{18,... | collective-permute-start | bytes 1179656 | tf_op jit(solution)/shard_map/ppermute | solution.py:25
  435.0 63.5 %collective-permute-start.57 = (bf16[2,64,2048]{2,1,0:T(8,128)(2,1)}, bf16[2,64,2048]{2,1,0:T(8,128)(2,1)}, u32[]{:S(2)}, u32[]{:S(2)}) collective-permute-start(bf16[2,64,2048]{2,1,0:T(8,128)(2,1)} %dynamic-slice_bitcast_fusion.3), channel_id=1, source_target_pairs={{0,8},{2,10},{4,12},{6,14},{8,0},{10,2},{12,4},{14,6},{16,24},{18,... | collective-permute-start | bytes 1572872 | tf_op jit(solution)/shard_map/ppermute | solution.py:25
  456.2 43.6 %collective-permute-start.61 = (bf16[2,64,2048]{2,1,0:T(8,128)(2,1)S(1)}, bf16[2,64,2048]{2,1,0:T(8,128)(2,1)S(1)}, u32[]{:S(2)}, u32[]{:S(2)}) collective-permute-start(bf16[2,64,2048]{2,1,0:T(8,128)(2,1)S(1)} %dynamic-slice_bitcast_fusion.2), channel_id=1, source_target_pairs={{0,16},{2,18},{4,20},{6,22},{8,24},{10,26},{12,28},{14,30},{16,0},... | collective-permute-start | bytes 1572872 | tf_op jit(solution)/shard_map/ppermute | solution.py:25
  464.2 28.7 %collective-permute-start.49 = (bf16[2,64,768]{2,1,0:T(8,128)(2,1)S(1)}, bf16[2,64,768]{2,1,0:T(8,128)(2,1)S(1)}, u32[]{:S(2)}, u32[]{:S(2)}) collective-permute-start(bf16[2,64,768]{2,1,0:T(8,128)(2,1)S(1)} %dynamic-slice_bitcast_fusion.9), channel_id=1, source_target_pairs={{0,16},{2,18},{4,20},{6,22},{8,24},{10,26},{12,28},{14,30},{16,0},... | collective-permute-start | bytes 589832 | tf_op jit(solution)/shard_map/ppermute | solution.py:25
  475.8 18.2 %collective-permute-start.46 = (bf16[64,768]{1,0:T(8,128)(2,1)S(1)}, bf16[64,768]{1,0:T(8,128)(2,1)S(1)}, u32[]{:S(2)}, u32[]{:S(2)}) collective-permute-start(bf16[64,768]{1,0:T(8,128)(2,1)S(1)} %dynamic-slice_bitcast_fusion.13), channel_id=1, source_target_pairs={{0,16},{2,18},{4,20},{6,22},{8,24},{10,26},{12,28},{14,30},{16,0},... | collective-permute-start | bytes 294920 | tf_op jit(solution)/shard_map/ppermute | solution.py:25
  (110 other events, 1508.8 us)
